TPU v7x, 32 devices: a whole 2x2x4 slice. The times are simulated.
32 devices in a mesh: section: 2 (over x), dp: 16 (over z, y, core).
Axes of the slice: x: 2, y: 2, z: 4, core: 2. Of those that a mesh axis runs over, the one named last changes fastest.
Arguments:
- hidden: bfloat16 [32, 256, 3584], P(('section', 'dp')), may hold values from -1000 to 1000, as said below
- lengths: int32 [32], P(('section', 'dp')), may hold values from 64 to 256, as said below
- pair_perm: int32 [16], replicated, may hold values from 0 to 15, as said below
- norm_gain: bfloat16 [3584], replicated, may hold values from 0.099609375 to 1.8984375
- projection: bfloat16 [3584, 1024], replicated, may hold values from -0.09375 to 0.09375
Outputs:
- hidden_grad: bfloat16 [32, 256, 3584], P(('section', 'dp'))
- loss: float32 [], replicated
Inputs may be any that keep to these rules, and one draw needn't show every extreme that they name: hidden rows of the encoder, finite. `lengths`: every sequence holds at least 64 valid tokens, and some sequence fills all 256 positions. `pair_perm`: a permutation: each docstring is paired with exactly one code.
All inputs are finite; a program needn't handle non-finite values.
Results may differ from a plain program's by a relative error of at most 0.008.
Values may be sent and summed in bfloat16 or wider, within the bound.
No kernel may reach another device: no remote copies, remote signals or barrier semaphores. Data moves between devices by JAX's collectives and lax.ppermute only.
A program may use at most 64 MiB of HBM per device.

v0:
```python
import jax
import jax.numpy as jnp
from jax import lax
from jax.sharding import PartitionSpec as P

inv_temp = 20.0
loss_scale = 1024.0
norm_eps = 1e-06


def partners(pair_perm):
    pair_count = pair_perm.shape[0]
    order_ids = jnp.arange(pair_count, dtype=jnp.int32)
    inverse = jnp.zeros((pair_count,), jnp.int32).at[pair_perm].set(order_ids)
    return jnp.concatenate([pair_perm + pair_count, inverse])


def contract_last(left_mat, right_mat):
    return lax.dot_general(
        left_mat, right_mat, (((1,), (1,)), ((), ())), preferred_element_type=jnp.float32
    )


def body(hidden, lengths, pair_perm, norm_gain, projection):
    seq_dev = hidden.shape[0]
    width = hidden.shape[2]
    seq_count = seq_dev * lax.axis_size(("section", "dp"))
    pair_count = seq_count // 2
    device = lax.axis_index(("section", "dp"))
    first_seq = device * seq_dev
    other_start = jnp.where(first_seq >= pair_count, 0, pair_count).astype(jnp.int32)
    gain_f = norm_gain.astype(jnp.float32)
    values = hidden.astype(jnp.float32)
    inv_rms = lax.rsqrt(jnp.mean(values * values, axis=2) + norm_eps)
    positions = jnp.arange(hidden.shape[1], dtype=jnp.int32)
    share = (positions[None, :] < lengths[:, None]).astype(jnp.float32) / lengths.astype(
        jnp.float32
    )[:, None]
    pooled = (jnp.sum((share * inv_rms)[:, :, None] * values, axis=1) * gain_f[None, :]).astype(
        jnp.bfloat16
    )
    raw_emb = jnp.dot(pooled, projection, preferred_element_type=jnp.float32)
    magnitude = jnp.sqrt(jnp.sum(raw_emb * raw_emb, axis=1, keepdims=True) + norm_eps)
    unit = raw_emb / magnitude
    own_emb = unit.astype(jnp.bfloat16)
    gathered = lax.all_gather(own_emb, ("section", "dp"), axis=0, tiled=True)
    others = lax.dynamic_slice_in_dim(gathered, other_start, pair_count, 0)
    scores = inv_temp * contract_last(own_emb, others)
    exp_scores = jnp.exp(scores)
    partner_own = lax.dynamic_slice_in_dim(partners(pair_perm), first_seq, seq_dev, 0) - other_start
    columns = jnp.arange(pair_count, dtype=jnp.int32)
    target = (columns[None, :] == partner_own[:, None]).astype(jnp.float32)
    target_scores = jnp.sum(target * scores, axis=1)
    totals = jnp.sum(exp_scores, axis=1)
    own_loss = jnp.sum(jnp.log(totals)) - jnp.sum(target_scores)
    loss = lax.psum(own_loss, ("section", "dp")) / seq_count
    all_totals = lax.all_gather(totals, ("section", "dp"), axis=0, tiled=True)
    other_totals = lax.dynamic_slice_in_dim(all_totals, other_start, pair_count, 0)
    factor = loss_scale * inv_temp
    factors = exp_scores / totals[:, None] + exp_scores / other_totals[None, :] - 2.0 * target
    demb = factor * jnp.dot(factors, others.astype(jnp.float32), precision=lax.Precision.HIGHEST)
    projected = jnp.sum(unit * demb, axis=1, keepdims=True)
    grad_raw = ((demb - unit * projected) / magnitude).astype(jnp.bfloat16)
    grad_pooled = contract_last(grad_raw, projection)
    scaled = grad_pooled * gain_f[None, :]
    dot_rows = jnp.sum(values * scaled[:, None, :], axis=2)
    result = share[:, :, None] * (
        inv_rms[:, :, None] * scaled[:, None, :]
        - values * (inv_rms**3 * dot_rows / width)[:, :, None]
    )
    return (result.astype(jnp.bfloat16), loss)


def solution(mesh):
    in_specs = (P(("section", "dp"), None, None), P(("section", "dp")), P(), P(), P())
    out_specs = (P(("section", "dp"), None, None), P())
    return jax.shard_map(body, mesh=mesh, in_specs=in_specs, out_specs=out_specs, check_vma=False)
```

profile of v0, /device:TPU:0, one launch (start us, length us, event | category | flops | bytes accessed | tf_op | source)
XLA Modules:
  0.0 108.2 jit_solution(9902439572852943731)
XLA Ops:
  0.6 0.0 copy-start.1
  1.4 1.9 %fusion = f32[256]{0:T(256)S(1)} fusion(bf16[1,256,3584]{2,1,0:T(8,128)(2,1)} %param.5), kind=kLoop, calls=%fused_computation.5 | loop fusion | flops 2752256 | bytes 1836032 | tf_op jit(solution)/shard_map/reduce_sum | solution.py:34
  3.3 0.7 broadcast_add_fusion
  4.0 0.6 scatter_custom_fusion
  4.6 0.1 pad_add_fusion
  4.7 0.6 dynamic_slice.11
  5.9 2.0 %fusion.1 = f32[3584]{0:T(1024)S(1)} fusion(bf16[1,256,3584]{2,1,0:T(8,128)(2,1)} %param.5, f32[256]{0:T(256)S(1)} %get-tuple-element.7), kind=kLoop, calls=%fused_computation.6 | loop fusion | flops 2748928 | bytes 1850368 | tf_op jit(solution)/shard_map/reduce_sum | solution.py:39
  7.9 0.0 copy-done.1
  8.0 4.1 %fusion.31 = f32[1,1024]{1,0:T(1,128)S(1)} fusion(bf16[3584,1]{0,1:T(2,128)(2,1)S(1)} %reshape.187, bf16[3584,1024]{1,0:T(8,128)(2,1)} %param.9), kind=kOutput, calls=%fused_computation.53 | convolution fusion | flops 7340032 | bytes 7351296 | tf_op jit(solution)/shard_map/dot_general | solution.py:42
  12.1 0.6 multiply_reduce_fusion.1
  13.4 43.4 %all-gather = bf16[32768]{0:T(1024)(128)(2,1)S(1)} all-gather(bf16[1024]{0:T(1024)(128)(2,1)S(1)} %fusion.30), channel_id=2, replica_groups=mesh['section'=2,'dp'=16] {'section','dp'}, dimensions={0}, use_global_device_ids=true | all-gather | bytes 67584 | tf_op jit(solution)/shard_map/all_gather | solution.py:46
  56.9 0.7 fusion.16
  58.9 0.7 dynamic-update-slice
  59.5 36.8 %all-reduce.1 = (f32[32]{0:T(128)S(1)}, f32[]{:T(128)}) all-reduce(f32[32]{0:T(128)S(1)} %dynamic-update-slice, f32[]{:T(128)S(6)} %sub.25), channel_id=1, replica_groups=mesh['section'=2,'dp'=16] {'section','dp'}, use_global_device_ids=true, to_apply=%add | all-reduce | flops 33 | bytes 264
  97.0 0.8 fusion.7
  97.8 0.6 multiply_reduce_fusion
  98.4 0.7 divide_convert_fusion
  99.1 0.0 copy-start
  99.1 5.2 %convolution_reduce_fusion = f32[3584]{0:T(1024)S(1)} fusion(bf16[1024,1]{0,1:T(2,128)(2,1)S(1)} %reshape.193, bf16[3584,1024]{1,0:T(8,128)(2,1)} %param.9), kind=kOutput, calls=%fused_computation.11 | convolution fusion | flops 7340032 | bytes 7356416 | tf_op jit(solution)/shard_map/dot_general | solution.py:19
  104.3 0.0 copy-done
  104.3 0.4 fusion.2
  104.8 2.2 %fusion.5 = bf16[1,256,3584]{2,1,0:T(8,128)(2,1)} fusion(bf16[1,256,3584]{2,1,0:T(8,128)(2,1)S(1)} %copy-done, f32[256]{0:T(256)S(1)} %fusion.12, f32[3584]{0:T(1024)S(1)} %convert_multiply_fusion.4, f32[256]{0:T(256)S(1)} %get-tuple-element.6, f32[256]{0:T(256)S(1)} %compare_select_fusion.1), kind=kLoop, calls=%fused_computation.10 | loop fusion | flops 5505024 | bytes 3687424 | tf_op jit(solution)/shard_map/convert_element_type | solution.py:71
  (12 shorter events, 0.1 us)
Async XLA Ops:
  0.6 7.3 %copy-start.1 = (bf16[3584]{0:T(1024)(128)(2,1)S(1)}, bf16[3584]{0:T(1024)(128)(2,1)}, u32[]{:S(2)}) copy-start(bf16[3584]{0:T(1024)(128)(2,1)} %param.8) | copy-start | bytes 21508
  99.1 5.3 %copy-start = (bf16[1,256,3584]{2,1,0:T(8,128)(2,1)S(1)}, bf16[1,256,3584]{2,1,0:T(8,128)(2,1)}, u32[]{:S(2)}) copy-start(bf16[1,256,3584]{2,1,0:T(8,128)(2,1)} %param.5) | copy-start | bytes 5505028
where the time goes:
time: 109 us; the launch traced here: 108 us
  blocking collectives  80.2 us (74%)
  matrix products  10.9 us (10%)
  other arithmetic  9.26 us (8%)
  between operations  5.85 us (5%)
  local copies, waits for them, and re-layouts  1.94 us (2%)
    all_gather x1, blocking collectives, body(): gathered = lax.all_gather(own_emb, ('section', 'dp'), axis=0, tiled=True)  43.4 us
    unnamed x1, blocking collectives  36.8 us
    dot_general x2, matrix products, contract_last(): lax.dot_general(left_mat, right_mat, (((1,), (1,)), ((), ())), preferred_...  5.96 us
    dot_general x1, matrix products, body(): raw_emb = jnp.dot(pooled, projection, preferred_element_type=jnp.float32)  4.14 us
    convert_element_type x1, other arithmetic, body(): return (result.astype(jnp.bfloat16), loss)  2.22 us

commit v1 on v0

v1 whole, which is shorter than its diff:
```python
import functools

import jax
import jax.numpy as jnp
from jax import lax
from jax.experimental import pallas as pl
from jax.experimental.pallas import tpu as pltpu
from jax.sharding import PartitionSpec as P

inv_temp = 20.0
loss_scale = 1024.0
norm_eps = 1e-06
both = ("section", "dp")

lane = 128
hidden_parts = 4
proj_rows = 512
out_rows = 64
group = 32
back_rows = 768
mxu_rows = 256


def parts_of(total, count):
    step = total // count
    return [pl.ds(i * step, step) for i in range(count)]


def tall_parts(total, tall_rows):
    cuts = [(at, min(tall_rows, total - at)) for at in range(0, total, tall_rows)]
    at, tall = cuts.pop()
    return cuts + [(at, tall // 2), (at + tall // 2, tall - tall // 2)]


def three_parts(x):
    high = x.astype(jnp.bfloat16).astype(jnp.float32)
    middle = (x - high).astype(jnp.bfloat16).astype(jnp.float32)
    low = (x - high - middle).astype(jnp.bfloat16).astype(jnp.float32)
    return high, middle, low


def pool_kernel(
    length_ref, gain_ref, hidden_ref, proj_ref,
    copies_ref, raw_ref, squares_ref, scale_ref, rows, weights,
    gain_at, rows_sem, weights_sem, gain_sem,
):
    seq_len, width = rows.shape
    emb_width = weights.shape[1]
    gain_copy = pltpu.make_async_copy(gain_ref, gain_at, gain_sem)
    row_cuts = parts_of(seq_len, hidden_parts)
    proj_cuts = tall_parts(width, proj_rows)
    row_copies = [
        pltpu.make_async_copy(hidden_ref.at[0, cut], rows.at[cut], rows_sem.at[i])
        for i, cut in enumerate(row_cuts)
    ]
    proj_copies = [
        pltpu.make_async_copy(
            proj_ref.at[pl.ds(*cut)], weights.at[pl.ds(*cut)], weights_sem.at[i]
        )
        for i, cut in enumerate(proj_cuts)
    ]
    for copy in row_copies + [gain_copy] + proj_copies[:3]:
        copy.start()

    tall = seq_len // hidden_parts
    for i, copy in enumerate(row_copies):
        copy.wait()
        for later in proj_copies[3 + 3 * i : 6 + 3 * i]:
            later.start()
        for start in range(i * tall, (i + 1) * tall, group):
            cut = pl.ds(start, group)
            squares = jnp.zeros((group, lane), jnp.float32)
            for k in range(0, width, lane):
                x = rows[cut, k : k + lane].astype(jnp.float32)
                squares = squares + x * x
            squares_ref[cut, :] = squares

    terms = jnp.concatenate(three_parts(squares_ref[...]), axis=1).astype(jnp.bfloat16)
    sums = lax.dot_general(
        jnp.ones((16, 3 * lane), jnp.bfloat16), terms, (((1,), (1,)), ((), ())),
        preferred_element_type=jnp.float32,
    )
    length = length_ref[0]
    one_share = 1.0 / jnp.full((1, 1), length, jnp.int32).astype(jnp.float32)
    position = lax.broadcasted_iota(jnp.int32, sums.shape, 1)
    share = jnp.where(position < length, one_share, 0.0)
    high, middle, low = three_parts(share * lax.rsqrt(sums / width + norm_eps))
    term = lax.broadcasted_iota(jnp.int32, sums.shape, 0)
    near = jnp.where(term == 0, high, jnp.where(term == 1, middle, jnp.where(term == 2, low, 0.0)))
    pooled = jnp.dot(near.astype(jnp.bfloat16), rows[...], preferred_element_type=jnp.float32)
    gain_copy.wait()
    scale = gain_at[...].astype(jnp.float32).reshape(1, width)
    scale_ref[...] = scale
    pooled = jnp.sum(pooled, axis=0, keepdims=True) * scale
    pooled = jnp.broadcast_to(pooled, (16, width)).astype(jnp.bfloat16)

    raw = jnp.zeros((16, emb_width), jnp.float32)
    for (at, deep), copy in zip(proj_cuts, proj_copies):
        copy.wait()
        raw = raw + jnp.dot(
            pooled[:, at : at + deep],
            weights[pl.ds(at, deep), :],
            preferred_element_type=jnp.float32,
        )
    raw_ref[...] = raw[:1]
    sheet = lax.broadcasted_iota(jnp.int32, (8, lane), 0)
    block = raw[:8, :lane]
    for k in range(1, emb_width // lane):
        block = jnp.where(sheet == k, raw[:8, k * lane : (k + 1) * lane], block)
    total = jnp.sum(jnp.sum(block * block, axis=1, keepdims=True), axis=0, keepdims=True)
    emb = (block * lax.rsqrt(total + norm_eps)).astype(jnp.bfloat16)
    copies_ref[...] = jnp.broadcast_to(emb[None], copies_ref.shape)


def grad_kernel(
    length_ref, held_ref, perm_ref, raw_ref, squares_ref, scale_ref, rows, weights,
    out_ref, loss_ref,
    wide, results, loss_at, results_sem, loss_sem,
):
    seq_len, width = rows.shape
    emb_width = weights.shape[1]
    seq_count = held_ref.shape[0]
    pair_count = perm_ref.shape[1]

    me = lax.axis_index(both)
    wide[...] = held_ref[...].astype(jnp.float32).reshape(wide.shape)
    sheets = emb_width // lane
    chunks = [wide[pl.ds(k, seq_count, stride=sheets), :] for k in range(sheets)]
    emb_f = jnp.concatenate(chunks, axis=1)
    emb = emb_f.astype(jnp.bfloat16)
    scores = inv_temp * lax.dot_general(
        emb, emb, (((1,), (1,)), ((), ())), preferred_element_type=jnp.float32
    )
    square = (seq_count, seq_count)
    row_id = lax.broadcasted_iota(jnp.int32, square, 0)
    col_id = lax.broadcasted_iota(jnp.int32, square, 1)
    across = (row_id < pair_count) != (col_id < pair_count)
    exp_scores = jnp.where(across, jnp.exp(jnp.where(across, scores, 0.0)), 0.0)
    totals = jnp.sum(exp_scores, axis=1, keepdims=True)
    own_col = jnp.sum(jnp.where(col_id == me, exp_scores, 0.0), axis=1, keepdims=True)
    own_total = jnp.sum(own_col, axis=0, keepdims=True)
    perm = perm_ref[...]
    pair_id = lax.broadcasted_iota(jnp.int32, perm.shape, 1)
    as_code = jnp.where(pair_id == me, perm + pair_count, 0)
    as_doc = jnp.where(perm == me - pair_count, pair_id, 0)
    partner = jnp.sum(
        jnp.where(me < pair_count, as_code, as_doc).astype(jnp.float32), axis=1, keepdims=True
    ).astype(jnp.int32)
    seq_id = lax.broadcasted_iota(jnp.int32, (seq_count, 1), 0)
    target = jnp.where(seq_id == partner, 2.0, 0.0)
    factors = own_col * (1.0 / own_total + 1.0 / totals) - target
    demb = (loss_scale * inv_temp) * jnp.sum(factors * emb_f, axis=0, keepdims=True)
    raw = raw_ref[...]
    magnitude = jnp.sqrt(jnp.sum(raw * raw, axis=1, keepdims=True) + norm_eps)
    unit = raw / magnitude
    projected = jnp.sum(unit * demb, axis=1, keepdims=True)
    grad_raw = (demb - unit * projected) / magnitude
    grad_raw = jnp.broadcast_to(grad_raw, (16, emb_width)).astype(jnp.bfloat16)

    own_row = grad_raw[:8].astype(jnp.float32)
    pieces = []
    for start in range(0, width, back_rows):
        middle = start + mxu_rows
        piece = lax.dot_general(
            grad_raw, weights[pl.ds(start, mxu_rows), :], (((1,), (1,)), ((), ())),
            preferred_element_type=jnp.float32,
        )
        pieces.append(piece[:8])
        for at in range(middle, min(start + back_rows, width), lane):
            part = jnp.zeros((lane // 8, 8, lane), jnp.float32)
            for k in range(0, emb_width, lane):
                block = weights[pl.ds(at, lane), k : k + lane].astype(jnp.float32)
                part = part + block.reshape(part.shape) * own_row[None, :, k : k + lane]
            piece = jnp.sum(part.reshape(lane, lane).T, axis=0, keepdims=True)
            pieces.append(jnp.broadcast_to(piece, (8, lane)))
    scaled = jnp.concatenate(pieces, axis=1) * scale_ref[...]

    matched = (row_id == perm_at_columns(perm, pair_count, seq_count)) & (col_id < pair_count)
    target_sum = jnp.sum(jnp.where(matched, scores, 0.0), axis=1, keepdims=True)
    terms = jnp.log(totals) - 2.0 * target_sum
    loss_at[...] = jnp.sum(terms, axis=0, keepdims=True) / seq_count
    loss_copy = pltpu.make_async_copy(loss_at, loss_ref, loss_sem)
    loss_copy.start()

    length = length_ref[0]
    one_share = 1.0 / jnp.full((1, 1), length, jnp.int32).astype(jnp.float32)
    mean = jnp.sum(squares_ref[...], axis=1, keepdims=True) / width
    inv_rms = lax.rsqrt(mean + norm_eps)
    position = lax.broadcasted_iota(jnp.int32, (seq_len, 1), 0)
    near_rows = jnp.where(position < length, one_share, 0.0) * inv_rms
    far_rows = near_rows * inv_rms * inv_rms / width

    nears, fars = [], []
    for start in range(0, seq_len, group):
        cut = pl.ds(start, group)
        dots = jnp.zeros((group // 8, 8, lane), jnp.float32)
        for k in range(0, width, lane):
            x = rows[cut, k : k + lane].astype(jnp.float32).reshape(dots.shape)
            dots = dots + x * scaled[None, :, k : k + lane]
        dot_rows = jnp.sum(dots.reshape(group, lane), axis=1, keepdims=True)
        far = far_rows[start : start + group] * dot_rows
        fars.append(jnp.broadcast_to(far, (group, lane)).reshape(dots.shape))
        near = near_rows[start : start + group]
        nears.append(jnp.broadcast_to(near, (group, lane)).reshape(dots.shape))

    out_copies = []
    for i, (at, tall) in enumerate(tall_parts(seq_len, out_rows)):
        rows_cut = pl.ds(at, tall)
        for start in range(at, at + tall, group):
            cut = pl.ds(start, group)
            near, far = nears[start // group], fars[start // group]
            for k in range(0, width, lane):
                x = rows[cut, k : k + lane].astype(jnp.float32).reshape(far.shape)
                result = near * scaled[None, :, k : k + lane] - far * x
                results[cut, k : k + lane] = result.reshape(group, lane).astype(jnp.bfloat16)
        out_copy = pltpu.make_async_copy(
            results.at[rows_cut], out_ref.at[0, rows_cut], results_sem.at[i]
        )
        out_copy.start()
        out_copies.append(out_copy)

    for out_copy in out_copies + [loss_copy]:
        out_copy.wait()


def perm_at_columns(perm, pair_count, seq_count):
    padding = jnp.full((1, seq_count - pair_count), -1, jnp.int32)
    return jnp.concatenate([perm + pair_count, padding], axis=1)


def body(hidden, lengths, pair_perm, norm_gain, projection):
    seq_len, width = hidden.shape[1:]
    emb_width = projection.shape[1]
    sheets = emb_width // lane
    seq_count = lax.axis_size(both)
    pair_count = seq_count // 2
    perm_row = pair_perm.reshape(1, pair_count)
    in_vmem = pl.BlockSpec(memory_space=pltpu.VMEM)
    anywhere = pl.BlockSpec(memory_space=pl.ANY)
    in_hbm = pl.BlockSpec(memory_space=pltpu.HBM)
    params = pltpu.CompilerParams(vmem_limit_bytes=16 * 1024 * 1024)
    copies, raw, squares, scale, rows, weights = pl.pallas_call(
        pool_kernel,
        out_shape=(
            pltpu.VMEM((seq_count, sheets, lane), jnp.bfloat16),
            pltpu.VMEM((1, emb_width), jnp.float32),
            pltpu.VMEM((seq_len, lane), jnp.float32),
            pltpu.VMEM((1, width), jnp.float32),
            pltpu.VMEM((seq_len, width), hidden.dtype),
            pltpu.VMEM((width, emb_width), projection.dtype),
        ),
        in_specs=[pl.BlockSpec(memory_space=pltpu.SMEM)] + [in_hbm] * 3,
        out_specs=(in_vmem,) * 6,
        scratch_shapes=[
            pltpu.VMEM((width,), norm_gain.dtype),
            pltpu.SemaphoreType.DMA((hidden_parts,)),
            pltpu.SemaphoreType.DMA((len(tall_parts(width, proj_rows)),)),
            pltpu.SemaphoreType.DMA,
        ],
        compiler_params=params,
        name="pool",
    )(lengths, *(
        pltpu.with_memory_space_constraint(x, pltpu.HBM)
        for x in (norm_gain, hidden, projection)
    ))

    held = lax.all_to_all(copies, both, 0, 0, tiled=True)

    grad, loss = pl.pallas_call(
        grad_kernel,
        out_shape=(
            jax.ShapeDtypeStruct(hidden.shape, jnp.bfloat16),
            jax.ShapeDtypeStruct((1, 1), jnp.float32),
        ),
        in_specs=[pl.BlockSpec(memory_space=pltpu.SMEM)] + [in_vmem] * 7,
        out_specs=(anywhere, anywhere),
        scratch_shapes=[
            pltpu.VMEM((seq_count * sheets, lane), jnp.float32),
            pltpu.VMEM((seq_len, width), jnp.bfloat16),
            pltpu.VMEM((1, 1), jnp.float32),
            pltpu.SemaphoreType.DMA((len(tall_parts(seq_len, out_rows)),)),
            pltpu.SemaphoreType.DMA,
        ],
        compiler_params=params,
        name="grad",
    )(lengths, *(
        pltpu.with_memory_space_constraint(x, pltpu.VMEM)
        for x in (held, perm_row, raw, squares, scale, rows, weights)
    ))
    return (grad, loss[0, 0])


def solution(mesh):
    in_specs = (P(both, None, None), P(both), P(), P(), P())
    out_specs = (P(both, None, None), P())
    return jax.shard_map(body, mesh=mesh, in_specs=in_specs, out_specs=out_specs, check_vma=False)
```

time: 109 us -> 23.7 us (0.22)
  blocking collectives: 80.2 us -> 14.5 us
  matrix products: 10.9 us -> 0 us
  other arithmetic: 9.26 us -> 0 us
  Pallas kernels: 0 us -> 7.68 us
  between operations: 5.85 us -> 1.29 us
  local copies, waits for them, and re-layouts: 1.94 us -> 0.01 us
    all_gather x1 -> x0, blocking collectives: 43.4 us -> none  [body(): gathered = lax.all_gather(own_emb, ('section', 'dp'), axis=0, tiled=True)]
    unnamed x1 -> x0, blocking collectives: 36.8 us -> none
    all_to_all x0 -> x1, blocking collectives: none -> 14.5 us  [body(): held = lax.all_to_all(copies, both, 0, 0, tiled=True)]
    dot_general x4 -> x0, matrix products: 10.9 us -> none  [the longest x2 5.96 us: contract_last(): lax.dot_general(left_mat, right_mat, (((1,), (1,)), ((), ())), preferred_...]
    pallas_call x0 -> x2, Pallas kernels: none -> 7.68 us  [the longest x1 4.23 us: body(): pl.pallas_call(pool_kernel, out_shape=(pltpu.VMEM((seq_count, sheets, lan...]
    reduce_sum x5 -> x0, other arithmetic: 5.61 us -> none  [the longest x1 1.99 us: body(): jnp.sum((share * inv_rms)[:, :, None] * values, axis=1) * gain_f[None, :]]
    convert_element_type x4 -> x0, other arithmetic: 2.89 us -> none  [the longest x1 2.22 us: body(): return (result.astype(jnp.bfloat16), loss)]
where the time goes in v1:
time: 23.7 us; the launch traced here: 23.5 us
  blocking collectives  14.5 us (61%)
  Pallas kernels  7.68 us (32%)
  between operations  1.29 us (5%)
    all_to_all x1, blocking collectives, body(): held = lax.all_to_all(copies, both, 0, 0, tiled=True)  14.5 us
    pallas_call x1, Pallas kernels, body(): pl.pallas_call(pool_kernel, out_shape=(pltpu.VMEM((seq_count, sheets, lan...  4.23 us
    pallas_call x1, Pallas kernels, body(): pl.pallas_call(grad_kernel, out_shape=(jax.ShapeDtypeStruct(hidden.shape,...  3.45 us

profile of v1, /device:TPU:0, one launch (start us, length us, event | category | flops | bytes accessed | tf_op | source)
XLA Modules:
  0.0 23.5 jit_solution(16943177159816153211)
XLA Ops:
  1.3 0.0 copy-start
  1.3 4.2 %pool.1 = (bf16[32,8,128]{2,1,0:T(8,128)(2,1)S(1)}, f32[1,1024]{1,0:T(1,128)S(1)}, f32[256,128]{1,0:T(8,128)S(1)}, f32[1,3584]{1,0:T(1,128)S(1)}, bf16[256,3584]...) custom-call(s32[1]{0:T(128)S(6)} %copy.7.length_ref, bf16[3584]{0:T(1024)(128)(2,1)} %gain_ref.1, ...), custom_call_target="tpu_custom_call" | custom-call | tf_op jit(solution)/shard_map/pool/pallas_call | solution.py:242
  5.5 14.5 %all_to_all.5.held_ref = bf16[32,8,128]{2,1,0:T(8,128)(2,1)S(1)} all-to-all(bf16[32,8,128]{2,1,0:T(8,128)(2,1)S(1)} %get-tuple-element.10), channel_id=1, replica_groups=mesh['section'=2,'dp'=16] {'section','dp'}, dimensions={0} | all-to-all | bytes 131072 | tf_op jit(solution)/shard_map/all_to_all | solution.py:267
  20.0 0.0 copy-done
  20.0 3.5 %grad.1 = (bf16[1,256,3584]{2,1,0:T(8,128)(2,1)}, f32[1,1]{1,0:T(1,128)}) custom-call(s32[1]{0:T(128)S(6)} %copy.7.length_ref, bf16[32,8,128]{2,1,0:T(8,128)(2,1)S(1)} %all_to_all.5.held_ref, s32[1,16]{1,0:T(1,128)S(1)} %bitcast.2, f32[1,1024]{1,0:T(1,128)S(1)} %get-tuple-element.11.raw_ref, f32[256,128]{1,0:T(8,128)S(1)} %get-tuple-element.12.squares_ref, ...), custom_call_target="tpu_custom_call" | custom-call | tf_op jit(solution)/shard_map/grad/pallas_call | solution.py:269
Async XLA Ops:
  1.3 18.8 %copy-start = (s32[16]{0:T(128)S(1)}, s32[16]{0:T(128)}, u32[]{:S(2)}) copy-start(s32[16]{0:T(128)} %param.7) | copy-start | bytes 196

commit v2 on v1

--- a/solution.py
+++ b/solution.py
@@ -14,10 +14,9 @@
 
 lane = 128
 hidden_parts = 4
-proj_rows = 512
-out_rows = 64
+tall_rows = 1024
 group = 32
-back_rows = 768
+back_parts = 4
 mxu_rows = 256
 
 
@@ -26,10 +25,15 @@
     return [pl.ds(i * step, step) for i in range(count)]
 
 
-def tall_parts(total, tall_rows):
+def tall_parts(total):
     cuts = [(at, min(tall_rows, total - at)) for at in range(0, total, tall_rows)]
     at, tall = cuts.pop()
     return cuts + [(at, tall // 2), (at + tall // 2, tall - tall // 2)]
+
+
+def out_cuts(total):
+    quarter = total // 4
+    return [(0, 2 * quarter), (2 * quarter, quarter), (3 * quarter, total - 3 * quarter)]
 
 
 def three_parts(x):
@@ -48,7 +52,7 @@
     emb_width = weights.shape[1]
     gain_copy = pltpu.make_async_copy(gain_ref, gain_at, gain_sem)
     row_cuts = parts_of(seq_len, hidden_parts)
-    proj_cuts = tall_parts(width, proj_rows)
+    proj_cuts = tall_parts(width)
     row_copies = [
         pltpu.make_async_copy(hidden_ref.at[0, cut], rows.at[cut], rows_sem.at[i])
         for i, cut in enumerate(row_cuts)
@@ -59,13 +63,13 @@
         )
         for i, cut in enumerate(proj_cuts)
     ]
-    for copy in row_copies + [gain_copy] + proj_copies[:3]:
+    for copy in row_copies + [gain_copy] + proj_copies[:1]:
         copy.start()
 
     tall = seq_len // hidden_parts
     for i, copy in enumerate(row_copies):
         copy.wait()
-        for later in proj_copies[3 + 3 * i : 6 + 3 * i]:
+        for later in proj_copies[1 + 2 * i : 3 + 2 * i]:
             later.start()
         for start in range(i * tall, (i + 1) * tall, group):
             cut = pl.ds(start, group)
@@ -159,14 +163,15 @@
 
     own_row = grad_raw[:8].astype(jnp.float32)
     pieces = []
-    for start in range(0, width, back_rows):
+    deep = width // back_parts
+    for start in range(0, width, deep):
         middle = start + mxu_rows
         piece = lax.dot_general(
             grad_raw, weights[pl.ds(start, mxu_rows), :], (((1,), (1,)), ((), ())),
             preferred_element_type=jnp.float32,
         )
         pieces.append(piece[:8])
-        for at in range(middle, min(start + back_rows, width), lane):
+        for at in range(middle, start + deep, lane):
             part = jnp.zeros((lane // 8, 8, lane), jnp.float32)
             for k in range(0, emb_width, lane):
                 block = weights[pl.ds(at, lane), k : k + lane].astype(jnp.float32)
@@ -204,7 +209,7 @@
         nears.append(jnp.broadcast_to(near, (group, lane)).reshape(dots.shape))
 
     out_copies = []
-    for i, (at, tall) in enumerate(tall_parts(seq_len, out_rows)):
+    for i, (at, tall) in enumerate(out_cuts(seq_len)):
         rows_cut = pl.ds(at, tall)
         for start in range(at, at + tall, group):
             cut = pl.ds(start, group)
@@ -254,7 +259,7 @@
         scratch_shapes=[
             pltpu.VMEM((width,), norm_gain.dtype),
             pltpu.SemaphoreType.DMA((hidden_parts,)),
-            pltpu.SemaphoreType.DMA((len(tall_parts(width, proj_rows)),)),
+            pltpu.SemaphoreType.DMA((len(tall_parts(width)),)),
             pltpu.SemaphoreType.DMA,
         ],
         compiler_params=params,
@@ -278,7 +283,7 @@
             pltpu.VMEM((seq_count * sheets, lane), jnp.float32),
             pltpu.VMEM((seq_len, width), jnp.bfloat16),
             pltpu.VMEM((1, 1), jnp.float32),
-            pltpu.SemaphoreType.DMA((len(tall_parts(seq_len, out_rows)),)),
+            pltpu.SemaphoreType.DMA((len(out_cuts(seq_len)),)),
             pltpu.SemaphoreType.DMA,
         ],
         compiler_params=params,

time: 23.7 us -> 23.9 us (level)
  no operation moved by 1% of the time
where the time goes in v2:
time: 23.9 us; the launch traced here: 23.7 us
  blocking collectives  14.5 us (61%)
  Pallas kernels  7.91 us (33%)
  between operations  1.29 us (5%)
    all_to_all x1, blocking collectives, body(): held = lax.all_to_all(copies, both, 0, 0, tiled=True)  14.5 us
    pallas_call x1, Pallas kernels, body(): pl.pallas_call(pool_kernel, out_shape=(pltpu.VMEM((seq_count, sheets, lan...  4.35 us
    pallas_call x1, Pallas kernels, body(): pl.pallas_call(grad_kernel, out_shape=(jax.ShapeDtypeStruct(hidden.shape,...  3.56 us

profile of v2, /device:TPU:0, one launch (start us, length us, event | category | flops | bytes accessed | tf_op | source)
XLA Modules:
  0.0 23.7 jit_solution(7175522090489652690)
XLA Ops:
  1.3 0.0 copy-start
  1.3 4.3 %pool.1 = (bf16[32,8,128]{2,1,0:T(8,128)(2,1)S(1)}, f32[1,1024]{1,0:T(1,128)S(1)}, f32[256,128]{1,0:T(8,128)S(1)}, f32[1,3584]{1,0:T(1,128)S(1)}, bf16[256,3584]...) custom-call(s32[1]{0:T(128)S(6)} %copy.7.length_ref, bf16[3584]{0:T(1024)(128)(2,1)} %gain_ref.1, ...), custom_call_target="tpu_custom_call" | custom-call | tf_op jit(solution)/shard_map/pool/pallas_call | solution.py:247
  5.6 14.5 %all_to_all.5.held_ref = bf16[32,8,128]{2,1,0:T(8,128)(2,1)S(1)} all-to-all(bf16[32,8,128]{2,1,0:T(8,128)(2,1)S(1)} %get-tuple-element.10), channel_id=1, replica_groups=mesh['section'=2,'dp'=16] {'section','dp'}, dimensions={0} | all-to-all | bytes 131072 | tf_op jit(solution)/shard_map/all_to_all | solution.py:272
  20.2 0.0 copy-done
  20.2 3.6 %grad.1 = (bf16[1,256,3584]{2,1,0:T(8,128)(2,1)}, f32[1,1]{1,0:T(1,128)}) custom-call(s32[1]{0:T(128)S(6)} %copy.7.length_ref, bf16[32,8,128]{2,1,0:T(8,128)(2,1)S(1)} %all_to_all.5.held_ref, s32[1,16]{1,0:T(1,128)S(1)} %bitcast.2, f32[1,1024]{1,0:T(1,128)S(1)} %get-tuple-element.11.raw_ref, f32[256,128]{1,0:T(8,128)S(1)} %get-tuple-element.12.squares_ref, ...), custom_call_target="tpu_custom_call" | custom-call | tf_op jit(solution)/shard_map/grad/pallas_call | solution.py:274
Async XLA Ops:
  1.3 18.9 %copy-start = (s32[16]{0:T(128)S(1)}, s32[16]{0:T(128)}, u32[]{:S(2)}) copy-start(s32[16]{0:T(128)} %param.7) | copy-start | bytes 196

commit v3 on v2

--- a/solution.py
+++ b/solution.py
@@ -14,7 +14,7 @@
 
 lane = 128
 hidden_parts = 4
-tall_rows = 1024
+tall_rows = 512
 group = 32
 back_parts = 4
 mxu_rows = 256
@@ -29,11 +29,6 @@
     cuts = [(at, min(tall_rows, total - at)) for at in range(0, total, tall_rows)]
     at, tall = cuts.pop()
     return cuts + [(at, tall // 2), (at + tall // 2, tall - tall // 2)]
-
-
-def out_cuts(total):
-    quarter = total // 4
-    return [(0, 2 * quarter), (2 * quarter, quarter), (3 * quarter, total - 3 * quarter)]
 
 
 def three_parts(x):
@@ -45,8 +40,8 @@
 
 def pool_kernel(
     length_ref, gain_ref, hidden_ref, proj_ref,
-    copies_ref, raw_ref, squares_ref, scale_ref, rows, weights,
-    gain_at, rows_sem, weights_sem, gain_sem,
+    copies_ref, raw_ref, near_ref, far_ref, scale_ref, rows, weights,
+    gain_at, squares_ref, rows_sem, weights_sem, gain_sem,
 ):
     seq_len, width = rows.shape
     emb_width = weights.shape[1]
@@ -63,13 +58,13 @@
         )
         for i, cut in enumerate(proj_cuts)
     ]
-    for copy in row_copies + [gain_copy] + proj_copies[:1]:
+    for copy in row_copies + [gain_copy] + proj_copies[:2]:
         copy.start()
 
     tall = seq_len // hidden_parts
     for i, copy in enumerate(row_copies):
         copy.wait()
-        for later in proj_copies[1 + 2 * i : 3 + 2 * i]:
+        for later in proj_copies[2 + 2 * i : 4 + 2 * i]:
             later.start()
         for start in range(i * tall, (i + 1) * tall, group):
             cut = pl.ds(start, group)
@@ -106,6 +101,13 @@
             weights[pl.ds(at, deep), :],
             preferred_element_type=jnp.float32,
         )
+        if at == 0:
+            mean = jnp.sum(squares_ref[...], axis=1, keepdims=True) / width
+            inv_rms = jnp.broadcast_to(lax.rsqrt(mean + norm_eps), (seq_len, lane))
+            position = lax.broadcasted_iota(jnp.int32, (seq_len, lane), 0)
+            near_rows = jnp.where(position < length, one_share, 0.0) * inv_rms
+            near_ref[...] = near_rows
+            far_ref[...] = near_rows * inv_rms * inv_rms / width
     raw_ref[...] = raw[:1]
     sheet = lax.broadcasted_iota(jnp.int32, (8, lane), 0)
     block = raw[:8, :lane]
@@ -117,7 +119,7 @@
 
 
 def grad_kernel(
-    length_ref, held_ref, perm_ref, raw_ref, squares_ref, scale_ref, rows, weights,
+    held_ref, perm_ref, raw_ref, near_ref, far_ref, scale_ref, rows, weights,
     out_ref, loss_ref,
     wide, results, loss_at, results_sem, loss_sem,
 ):
@@ -125,6 +127,7 @@
     emb_width = weights.shape[1]
     seq_count = held_ref.shape[0]
     pair_count = perm_ref.shape[1]
+    row_cuts = parts_of(seq_len, hidden_parts)
 
     me = lax.axis_index(both)
     wide[...] = held_ref[...].astype(jnp.float32).reshape(wide.shape)
@@ -187,14 +190,6 @@
     loss_copy = pltpu.make_async_copy(loss_at, loss_ref, loss_sem)
     loss_copy.start()
 
-    length = length_ref[0]
-    one_share = 1.0 / jnp.full((1, 1), length, jnp.int32).astype(jnp.float32)
-    mean = jnp.sum(squares_ref[...], axis=1, keepdims=True) / width
-    inv_rms = lax.rsqrt(mean + norm_eps)
-    position = lax.broadcasted_iota(jnp.int32, (seq_len, 1), 0)
-    near_rows = jnp.where(position < length, one_share, 0.0) * inv_rms
-    far_rows = near_rows * inv_rms * inv_rms / width
-
     nears, fars = [], []
     for start in range(0, seq_len, group):
         cut = pl.ds(start, group)
@@ -203,15 +198,14 @@
             x = rows[cut, k : k + lane].astype(jnp.float32).reshape(dots.shape)
             dots = dots + x * scaled[None, :, k : k + lane]
         dot_rows = jnp.sum(dots.reshape(group, lane), axis=1, keepdims=True)
-        far = far_rows[start : start + group] * dot_rows
-        fars.append(jnp.broadcast_to(far, (group, lane)).reshape(dots.shape))
-        near = near_rows[start : start + group]
-        nears.append(jnp.broadcast_to(near, (group, lane)).reshape(dots.shape))
-
+        far = far_ref[cut, :] * jnp.broadcast_to(dot_rows, (group, lane))
+        fars.append(far.reshape(dots.shape))
+        nears.append(near_ref[cut, :].reshape(dots.shape))
+
+    tall = seq_len // hidden_parts
     out_copies = []
-    for i, (at, tall) in enumerate(out_cuts(seq_len)):
-        rows_cut = pl.ds(at, tall)
-        for start in range(at, at + tall, group):
+    for i, rows_cut in enumerate(row_cuts):
+        for start in range(i * tall, (i + 1) * tall, group):
             cut = pl.ds(start, group)
             near, far = nears[start // group], fars[start // group]
             for k in range(0, width, lane):
@@ -244,20 +238,22 @@
     anywhere = pl.BlockSpec(memory_space=pl.ANY)
     in_hbm = pl.BlockSpec(memory_space=pltpu.HBM)
     params = pltpu.CompilerParams(vmem_limit_bytes=16 * 1024 * 1024)
-    copies, raw, squares, scale, rows, weights = pl.pallas_call(
+    copies, raw, near, far, scale, rows, weights = pl.pallas_call(
         pool_kernel,
         out_shape=(
             pltpu.VMEM((seq_count, sheets, lane), jnp.bfloat16),
             pltpu.VMEM((1, emb_width), jnp.float32),
+            pltpu.VMEM((seq_len, lane), jnp.float32),
             pltpu.VMEM((seq_len, lane), jnp.float32),
             pltpu.VMEM((1, width), jnp.float32),
             pltpu.VMEM((seq_len, width), hidden.dtype),
             pltpu.VMEM((width, emb_width), projection.dtype),
         ),
         in_specs=[pl.BlockSpec(memory_space=pltpu.SMEM)] + [in_hbm] * 3,
-        out_specs=(in_vmem,) * 6,
+        out_specs=(in_vmem,) * 7,
         scratch_shapes=[
             pltpu.VMEM((width,), norm_gain.dtype),
+            pltpu.VMEM((seq_len, lane), jnp.float32),
             pltpu.SemaphoreType.DMA((hidden_parts,)),
             pltpu.SemaphoreType.DMA((len(tall_parts(width)),)),
             pltpu.SemaphoreType.DMA,
@@ -277,20 +273,20 @@
             jax.ShapeDtypeStruct(hidden.shape, jnp.bfloat16),
             jax.ShapeDtypeStruct((1, 1), jnp.float32),
         ),
-        in_specs=[pl.BlockSpec(memory_space=pltpu.SMEM)] + [in_vmem] * 7,
+        in_specs=[in_vmem] * 8,
         out_specs=(anywhere, anywhere),
         scratch_shapes=[
             pltpu.VMEM((seq_count * sheets, lane), jnp.float32),
             pltpu.VMEM((seq_len, width), jnp.bfloat16),
             pltpu.VMEM((1, 1), jnp.float32),
-            pltpu.SemaphoreType.DMA((len(out_cuts(seq_len)),)),
+            pltpu.SemaphoreType.DMA((hidden_parts,)),
             pltpu.SemaphoreType.DMA,
         ],
         compiler_params=params,
         name="grad",
-    )(lengths, *(
+    )(*(
         pltpu.with_memory_space_constraint(x, pltpu.VMEM)
-        for x in (held, perm_row, raw, squares, scale, rows, weights)
+        for x in (held, perm_row, raw, near, far, scale, rows, weights)
     ))
     return (grad, loss[0, 0])
 

time: 23.9 us -> 23.6 us (0.987)
  Pallas kernels: 7.91 us -> 7.67 us
where the time goes in v3:
time: 23.6 us; the launch traced here: 23.5 us
  blocking collectives  14.5 us (61%)
  Pallas kernels  7.67 us (32%)
  between operations  1.29 us (5%)
    all_to_all x1, blocking collectives, body(): held = lax.all_to_all(copies, both, 0, 0, tiled=True)  14.5 us
    pallas_call x1, Pallas kernels, body(): pl.pallas_call(pool_kernel, out_shape=(pltpu.VMEM((seq_count, sheets, lan...  4.21 us
    pallas_call x1, Pallas kernels, body(): pl.pallas_call(grad_kernel, out_shape=(jax.ShapeDtypeStruct(hidden.shape,...  3.46 us

profile of v3, /device:TPU:0, one launch (start us, length us, event | category | flops | bytes accessed | tf_op | source)
XLA Modules:
  0.0 23.5 jit_solution(9098108657558101671)
XLA Ops:
  1.3 0.0 copy-start
  1.3 4.2 %pool.1 = (bf16[32,8,128]{2,1,0:T(8,128)(2,1)S(1)}, f32[1,1024]{1,0:T(1,128)S(1)}, f32[256,128]{1,0:T(8,128)S(1)}, f32[256,128]{1,0:T(8,128)S(1)}, f32[1,3584]{1...) custom-call(s32[1]{0:T(128)S(6)} %copy.7.length_ref, bf16[3584]{0:T(1024)(128)(2,1)} %gain_ref.1, ...), custom_call_target="tpu_custom_call" | custom-call | tf_op jit(solution)/shard_map/pool/pallas_call | solution.py:241
  5.5 14.5 %all_to_all.5.held_ref = bf16[32,8,128]{2,1,0:T(8,128)(2,1)S(1)} all-to-all(bf16[32,8,128]{2,1,0:T(8,128)(2,1)S(1)} %get-tuple-element.11), channel_id=1, replica_groups=mesh['section'=2,'dp'=16] {'section','dp'}, dimensions={0} | all-to-all | bytes 131072 | tf_op jit(solution)/shard_map/all_to_all | solution.py:268
  20.0 0.0 copy-done
  20.0 3.5 %grad.1 = (bf16[1,256,3584]{2,1,0:T(8,128)(2,1)}, f32[1,1]{1,0:T(1,128)}) custom-call(bf16[32,8,128]{2,1,0:T(8,128)(2,1)S(1)} %all_to_all.5.held_ref, s32[1,16]{1,0:T(1,128)S(1)} %bitcast.2, f32[1,1024]{1,0:T(1,128)S(1)} %get-tuple-element.12.raw_ref, f32[256,128]{1,0:T(8,128)S(1)} %get-tuple-element.13.near_ref, f32[256,128]{1,0:T(8,128)S(1)} %get-tuple-element.14.far_ref, ...), custom_call_target="tpu_custom_call" | custom-call | tf_op jit(solution)/shard_map/grad/pallas_call | solution.py:270
Async XLA Ops:
  1.3 18.7 %copy-start = (s32[16]{0:T(128)S(1)}, s32[16]{0:T(128)}, u32[]{:S(2)}) copy-start(s32[16]{0:T(128)} %param.7) | copy-start | bytes 196

commit v4 on v2

--- a/solution.py
+++ b/solution.py
@@ -14,7 +14,7 @@
 
 lane = 128
 hidden_parts = 4
-tall_rows = 1024
+tall_rows = 512
 group = 32
 back_parts = 4
 mxu_rows = 256
@@ -32,8 +32,8 @@
 
 
 def out_cuts(total):
-    quarter = total // 4
-    return [(0, 2 * quarter), (2 * quarter, quarter), (3 * quarter, total - 3 * quarter)]
+    tall = 2 * group
+    return [(0, group), (group, group)] + [(at, tall) for at in range(tall, total, tall)]
 
 
 def three_parts(x):
@@ -63,13 +63,13 @@
         )
         for i, cut in enumerate(proj_cuts)
     ]
-    for copy in row_copies + [gain_copy] + proj_copies[:1]:
+    for copy in row_copies + [gain_copy] + proj_copies[:2]:
         copy.start()
 
     tall = seq_len // hidden_parts
     for i, copy in enumerate(row_copies):
         copy.wait()
-        for later in proj_copies[1 + 2 * i : 3 + 2 * i]:
+        for later in proj_copies[2 + 2 * i : 4 + 2 * i]:
             later.start()
         for start in range(i * tall, (i + 1) * tall, group):
             cut = pl.ds(start, group)
@@ -96,9 +96,9 @@
     scale = gain_at[...].astype(jnp.float32).reshape(1, width)
     scale_ref[...] = scale
     pooled = jnp.sum(pooled, axis=0, keepdims=True) * scale
-    pooled = jnp.broadcast_to(pooled, (16, width)).astype(jnp.bfloat16)
-
-    raw = jnp.zeros((16, emb_width), jnp.float32)
+    pooled = jnp.broadcast_to(pooled, (8, width)).astype(jnp.bfloat16)
+
+    raw = jnp.zeros((8, emb_width), jnp.float32)
     for (at, deep), copy in zip(proj_cuts, proj_copies):
         copy.wait()
         raw = raw + jnp.dot(
@@ -159,7 +159,7 @@
     unit = raw / magnitude
     projected = jnp.sum(unit * demb, axis=1, keepdims=True)
     grad_raw = (demb - unit * projected) / magnitude
-    grad_raw = jnp.broadcast_to(grad_raw, (16, emb_width)).astype(jnp.bfloat16)
+    grad_raw = jnp.broadcast_to(grad_raw, (8, emb_width)).astype(jnp.bfloat16)
 
     own_row = grad_raw[:8].astype(jnp.float32)
     pieces = []

time: 23.9 us -> 23.7 us (level)
  no operation moved by 1% of the time
where the time goes in v4:
time: 23.7 us; the launch traced here: 23.5 us
  blocking collectives  14.5 us (61%)
  Pallas kernels  7.69 us (32%)
  between operations  1.29 us (5%)
    all_to_all x1, blocking collectives, body(): held = lax.all_to_all(copies, both, 0, 0, tiled=True)  14.5 us
    pallas_call x1, Pallas kernels, body(): pl.pallas_call(pool_kernel, out_shape=(pltpu.VMEM((seq_count, sheets, lan...  4.21 us
    pallas_call x1, Pallas kernels, body(): pl.pallas_call(grad_kernel, out_shape=(jax.ShapeDtypeStruct(hidden.shape,...  3.48 us

profile of v4, /device:TPU:0, one launch (start us, length us, event | category | flops | bytes accessed | tf_op | source)
XLA Modules:
  0.0 23.5 jit_solution(10264488900625123635)
XLA Ops:
  1.3 0.0 copy-start
  1.3 4.2 %pool.1 = (bf16[32,8,128]{2,1,0:T(8,128)(2,1)S(1)}, f32[1,1024]{1,0:T(1,128)S(1)}, f32[256,128]{1,0:T(8,128)S(1)}, f32[1,3584]{1,0:T(1,128)S(1)}, bf16[256,3584]...) custom-call(s32[1]{0:T(128)S(6)} %copy.7.length_ref, bf16[3584]{0:T(1024)(128)(2,1)} %gain_ref.1, ...), custom_call_target="tpu_custom_call" | custom-call | tf_op jit(solution)/shard_map/pool/pallas_call | solution.py:247
  5.5 14.5 %all_to_all.5.held_ref = bf16[32,8,128]{2,1,0:T(8,128)(2,1)S(1)} all-to-all(bf16[32,8,128]{2,1,0:T(8,128)(2,1)S(1)} %get-tuple-element.10), channel_id=1, replica_groups=mesh['section'=2,'dp'=16] {'section','dp'}, dimensions={0} | all-to-all | bytes 131072 | tf_op jit(solution)/shard_map/all_to_all | solution.py:272
  20.0 0.0 copy-done
  20.0 3.5 %grad.1 = (bf16[1,256,3584]{2,1,0:T(8,128)(2,1)}, f32[1,1]{1,0:T(1,128)}) custom-call(s32[1]{0:T(128)S(6)} %copy.7.length_ref, bf16[32,8,128]{2,1,0:T(8,128)(2,1)S(1)} %all_to_all.5.held_ref, s32[1,16]{1,0:T(1,128)S(1)} %bitcast.2, f32[1,1024]{1,0:T(1,128)S(1)} %get-tuple-element.11.raw_ref, f32[256,128]{1,0:T(8,128)S(1)} %get-tuple-element.12.squares_ref, ...), custom_call_target="tpu_custom_call" | custom-call | tf_op jit(solution)/shard_map/grad/pallas_call | solution.py:274
Async XLA Ops:
  1.3 18.7 %copy-start = (s32[16]{0:T(128)S(1)}, s32[16]{0:T(128)}, u32[]{:S(2)}) copy-start(s32[16]{0:T(128)} %param.7) | copy-start | bytes 196
